TPU v7x, 32 devices: a whole 2x2x4 slice. The times are simulated.
32 devices in a mesh: segment: 2 (over x), frames: 16 (over z, y, core).
Axes of the slice: x: 2, y: 2, z: 4, core: 2. Of those that a mesh axis runs over, the one named last changes fastest.
Arguments:
- hidden: bfloat16 [2, 4096, 1536], P('segment', 'frames'), may hold values from -3 to 3
- features: bfloat16 [1024, 768], P('frames'), may hold values from -160 to 160, as said below
- kv_weight: bfloat16 [2, 768, 3072], P('segment', None, 'frames'), may hold values from -0.21875 to 0.21875
- mod_table: float32 [2, 32, 3, 1536], P('segment'), may hold values from -4 to 4
- timestep: int32 [2, 64], P('segment', 'frames'), may hold values from 0 to 31
- block_list: int32 [2, 64, 4], P('segment', 'frames'), may hold values from 0 to 15
- block_count: int32 [2, 64], P('segment', 'frames'), may hold values from 1 to 4, as said below
Outputs:
- handed: bfloat16 [2, 4096, 1536], P('segment', 'frames')
Inputs may be any that keep to these rules, and one draw needn't show every extreme that they name: `features`: drawn as normal values, rows may carry common scales; within the bounds given. `block_list`: entry j of a block's list counts when j < the block's count; the others are ignored. `block_count`: the 4 frame blocks of one device have at most 10 live list entries together, and in every section some device has exactly 10.
All inputs are finite; a program needn't handle non-finite values.
Results may differ from a plain program's by a relative error of at most 0.0044.
The roundings to bfloat16 on the way count: a program that leaves them out, or rounds other values in their place, can miss the bound.
Values may be sent and summed in bfloat16 or wider, within the bound.
A program may use at most 64 MiB of HBM per device.

v0:
```python
import jax
import jax.numpy as jnp
from jax import lax
from jax.sharding import PartitionSpec as P

HEADS = 12
HD = 128
BLK = 64


def from_behind(block, axis, distance):
    devices = range(lax.axis_size(axis))
    route = [((i - distance) % len(devices), i) for i in devices]
    return lax.ppermute(block, axis, route)


def local(hidden, features, kv_weight, mod_table, timestep, block_list, block_count):
    feature_table = lax.all_gather(features, "frames", axis=0, tiled=True)
    stream = hidden[0].astype(jnp.float32)
    tok_rows = stream.shape[0]
    feature_width = stream.shape[1]
    blocks_here = tok_rows // BLK
    normed = stream * lax.rsqrt(jnp.mean(stream * stream, axis=-1, keepdims=True) + 1e-06)
    levels = mod_table.shape[1]
    onehot = (timestep[0][:, None] == jnp.arange(levels, dtype=jnp.int32)[None, :]).astype(
        jnp.float32
    )
    modulate = jnp.sum(onehot[:, :, None, None] * mod_table[0][None], axis=1)
    normed_blocks = normed.reshape(blocks_here, BLK, feature_width)
    queries = (
        normed_blocks * (1.0 + modulate[:, 1][:, None, :]) + modulate[:, 0][:, None, :]
    ).astype(jnp.bfloat16)
    queries = queries.reshape(blocks_here, BLK, HEADS, HD)
    list_counts = block_count[0]
    list_blocks = block_list[0]
    slot_count = list_blocks.shape[1]
    offsets = jnp.arange(BLK, dtype=jnp.int32)
    inv_root = 1.0 / HD**0.5
    row_index = (list_blocks[:, :, None] * BLK + offsets[None, None, :]).reshape(-1)
    key_mask = jnp.repeat(
        jnp.arange(slot_count, dtype=jnp.int32)[None, :] < list_counts[:, None], BLK, axis=1
    )
    selected = jnp.take(feature_table, row_index, axis=0)
    key_values = jnp.dot(
        selected,
        lax.all_gather(kv_weight[0], "frames", axis=1, tiled=True),
        preferred_element_type=jnp.float32,
    ).astype(jnp.bfloat16)
    key_heads = key_values[:, :feature_width].reshape(-1, HEADS, HD)
    value_heads = key_values[:, feature_width:].reshape(-1, HEADS, HD)
    keys_part = key_heads.reshape(blocks_here, -1, HEADS, HD)
    values_part = value_heads.reshape(blocks_here, -1, HEADS, HD)
    scores = jnp.einsum("bqhd,bkhd->bhqk", queries, keys_part, preferred_element_type=jnp.float32)
    softmax_scores = scores
    softmax_scores = jnp.where(
        key_mask[:, None, None, :], softmax_scores * inv_root, jnp.float32(-1e30)
    )
    top_score = jnp.max(softmax_scores, axis=-1, keepdims=True)
    expo = jnp.exp(softmax_scores - top_score)
    weights = (expo / jnp.sum(expo, axis=-1, keepdims=True)).astype(jnp.bfloat16)
    mixed_heads = jnp.einsum(
        "bhqk,bkhd->bqhd", weights, values_part, preferred_element_type=jnp.float32
    )
    part_blocks = blocks_here - 0
    mixed_rows = mixed_heads.reshape(part_blocks * BLK, feature_width)
    gate_rows = jnp.repeat(modulate[0:blocks_here, 2], BLK, axis=0)
    result = (stream + gate_rows * mixed_rows).astype(jnp.bfloat16)
    handed = from_behind(result[None], "segment", 1)
    return handed


def solution(mesh):
    placed = (
        P("segment", "frames", None),
        P("frames", None),
        P("segment", None, "frames"),
        P("segment", None, None, None),
        P("segment", "frames"),
        P("segment", "frames", None),
        P("segment", "frames"),
    )
    return jax.shard_map(
        local, mesh=mesh, in_specs=placed, out_specs=P("segment", "frames", None), check_vma=False
    )
```

profile of v0, /device:TPU:0, one launch (start us, length us, event | category | flops | bytes accessed | tf_op | source)
XLA Modules:
  0.0 167.4 jit_solution(1845038613848834141)
XLA Ops:
  6.5 0.0 copy-start
  6.5 0.0 copy-start.4
  6.5 0.0 copy-start.3
  6.5 0.0 copy-start.5
  6.5 0.0 all-gather.4.cloned.1.call-start
  6.6 0.7 all-gather.4.cloned.1.call-update
  7.3 0.0 all-gather.6.cloned.1.call-start
  7.3 0.7 all-gather.6.cloned.1.call-update
  8.0 0.7 multiply_bitcast_fusion
  8.7 0.1 iota_add_fusion
  8.8 0.1 add.89
  8.9 0.1 add.86
  8.9 1.6 reshape.134
  10.5 0.0 copy-done.4
  10.5 0.1 fusion.21
  10.6 0.0 copy-done.3
  10.6 0.4 multiply_reduce_fusion
  11.0 0.2 fusion.20
  11.2 0.0 copy-done
  11.2 0.2 multiply_reduce_fusion.1
  11.4 0.1 rsqrt.12
  11.5 0.0 copy-done.5
  11.5 0.1 iota_compare_fusion
  11.6 0.1 broadcast_in_dim.41
  11.7 0.1 broadcast_in_dim.42
  11.8 1.4 add_convert_fusion
  13.2 38.9 %all-gather.4.cloned.1.call-done = bf16[1024,768]{1,0:T(8,128)(2,1)} async-done(((bf16[64,768]{1,0:T(8,128)(2,1)}), bf16[1024,768]{1,0:T(8,128)(2,1)}) %all-gather.4.cloned.1.call-update) | async-done | bytes 1572880 | tf_op jit(solution)/shard_map/all_gather | solution.py:18
  52.1 6.1 %gather_fusion = bf16[1024,768]{1,0:T(8,128)(2,1)S(1)} fusion(bf16[1024,768]{1,0:T(8,128)(2,1)} %all-gather.4.cloned.1.call-done, s32[1024]{0:T(1024)S(1)} %broadcast_clamp_fusion), kind=kCustom, calls=%fused_computation | custom fusion | bytes 3149824 | tf_op jit(solution)/shard_map/jit(_take)/gather | solution.py:43
  58.2 48.5 %all-gather.6.cloned.1.call-done = bf16[1,768,3072]{1,2,0:T(8,128)(2,1)} async-done(((bf16[1,768,192]{1,2,0:T(8,128)(2,1)}), bf16[1,768,3072]{1,2,0:T(8,128)(2,1)}) %all-gather.6.cloned.1.call-update) | async-done | bytes 4718608 | tf_op jit(solution)/shard_map/all_gather | solution.py:46
  106.7 7.9 %convolution_convert_fusion = bf16[1024,3072]{1,0:T(8,128)(2,1)S(1)} fusion(bf16[1,768,3072]{1,2,0:T(8,128)(2,1)} %all-gather.6.cloned.1.call-done, bf16[1024,768]{1,0:T(8,128)(2,1)S(1)} %gather_fusion, pred[1024]{0:T(1024)(128)(4,1)S(1)} %compare_and_fusion), kind=kOutput, calls=%fused_computation.2 | convolution fusion | flops 4835770368 | bytes 12583936 | tf_op jit(solution)/shard_map/dot_general | solution.py:44
  114.6 2.2 %fusion.25 = (bf16[1024,1536]{1,0:T(8,128)(2,1)S(1)}, bf16[1024,1536]{1,0:T(8,128)(2,1)}) fusion(bf16[1024,3072]{1,0:T(8,128)(2,1)S(1)} %convolution_convert_fusion), kind=kLoop, calls=%fused_computation.44 | loop fusion | bytes 12582912 | tf_op jit(solution)/shard_map/slice | solution.py:49
  116.8 6.9 %reshape.144 = bf16[4,256,12,128]{3,2,1,0:T(8,128)(2,1)} reshape(bf16[1024,1536]{1,0:T(8,128)(2,1)} %get-tuple-element.8) | data formatting | bytes 6291456 | tf_op jit(solution)/shard_map/reshape;reshape | solution.py:52
  123.6 3.6 %reshape.145 = bf16[4,256,12,128]{3,2,1,0:T(8,128)(2,1)} reshape(bf16[1024,1536]{1,0:T(8,128)(2,1)S(1)} %get-tuple-element.7) | data formatting | bytes 6291456 | tf_op jit(solution)/shard_map/reshape;reshape | solution.py:51
  127.3 3.7 %fusion.2 = f32[4,12,64,256]{3,2,1,0:T(8,128)S(1)} fusion(bf16[4,256,12,128]{3,2,1,0:T(8,128)(2,1)} %reshape.145, bf16[4,64,12,128]{3,2,1,0:T(8,128)(2,1)} %add_convert_fusion), kind=kOutput, calls=%fused_computation.4 | convolution fusion | flops 201326592 | bytes 7077888 | tf_op jit(solution)/shard_map/bqhd,bkhd->bhqk/dot_general | solution.py:53
  131.0 0.0 copy-start.2
  131.0 1.4 fusion.26
  132.4 0.8 copy-done.2
  133.2 2.4 %fusion.15 = f32[4,64,12,128]{3,1,2,0:T(8,128)S(1)} fusion(bf16[4,256,12,128]{3,2,1,0:T(8,128)(2,1)S(1)} %copy-done.2, f32[4,12,64,256]{3,2,1,0:T(8,128)S(1)} %get-tuple-element.11, f32[4,12,64]{2,1,0:T(8,128)S(1)} %get-tuple-element.10), kind=kOutput, calls=%fused_computation.24 | convolution fusion | flops 202899456 | bytes 7876608 | tf_op jit(solution)/shard_map/bhqk,bkhd->bqhd/dot_general | solution.py:61
  135.6 0.9 copy.24
  136.6 0.0 copy-start.1
  136.6 1.4 reshape.133
  138.0 0.2 broadcast_in_dim.38
  138.1 0.0 copy-done.1
  138.1 1.8 %fusion.8 = bf16[1,256,1536]{2,1,0:T(8,128)(2,1)S(1)} fusion(f32[1,256,1536]{2,1,0:T(8,128)} %reshape.133, bf16[1,256,1536]{2,1,0:T(8,128)(2,1)S(1)} %copy-done.1, f32[1,256,1536]{2,1,0:T(8,128)S(1)} %bitcast.21), kind=kLoop, calls=%fused_computation.16 | loop fusion | flops 1572864 | bytes 4718592 | tf_op jit(solution)/shard_map/convert_element_type | solution.py:67
  139.9 1.5 collective-permute-start
  141.5 18.2 %collective-permute-done = bf16[1,256,1536]{2,1,0:T(8,128)(2,1)S(1)} collective-permute-done((bf16[1,256,1536]{2,1,0:T(8,128)(2,1)S(1)}, bf16[1,256,1536]{2,1,0:T(8,128)(2,1)S(1)}, u32[]{:S(2)}, u32[]{:S(2)}) %collective-permute-start) | collective-permute-done | bytes 786464 | tf_op jit(solution)/shard_map/ppermute | solution.py:14
  159.7 0.9 copy.41
  (7 shorter events, 0.1 us)
Async XLA Ops:
  6.5 4.6 %copy-start = (bf16[1,256,1536]{2,1,0:T(8,128)(2,1)S(1)}, bf16[1,256,1536]{2,1,0:T(8,128)(2,1)}, u32[]{:S(2)}) copy-start(bf16[1,256,1536]{2,1,0:T(8,128)(2,1)} %param.7) | copy-start | bytes 2359300
  6.5 4.0 %copy-start.4 = (s32[1,4]{1,0:T(1,128)S(1)}, s32[1,4]{1,0:T(1,128)}, u32[]{:S(2)}) copy-start(s32[1,4]{1,0:T(1,128)} %param.11) | copy-start | bytes 52
  6.5 4.1 %copy-start.3 = (f32[1,32,3,1536]{3,1,2,0:T(8,128)S(1)}, f32[1,32,3,1536]{3,1,2,0:T(8,128)}, u32[]{:S(2)}) copy-start(f32[1,32,3,1536]{3,1,2,0:T(8,128)} %param.10) | copy-start | bytes 1769476
  6.5 5.0 %copy-start.5 = (s32[1,4]{1,0:T(1,128)S(1)}, s32[1,4]{1,0:T(1,128)}, u32[]{:S(2)}) copy-start(s32[1,4]{1,0:T(1,128)} %param.13) | copy-start | bytes 52
  6.5 45.6 %all-gather.4.cloned.1.call-start = ((), (), s32[]{:S(2)}) async-start(), calls=%async_computation | async-start | bytes 1671168 | tf_op jit(solution)/shard_map/all_gather | solution.py:18
  7.3 99.4 %all-gather.6.cloned.1.call-start = ((), (), s32[]{:S(2)}) async-start(), calls=%async_computation.1 | async-start | bytes 5013504 | tf_op jit(solution)/shard_map/all_gather | solution.py:46
  131.0 2.2 %copy-start.2 = (bf16[4,256,12,128]{3,2,1,0:T(8,128)(2,1)S(1)}, bf16[4,256,12,128]{3,2,1,0:T(8,128)(2,1)}, u32[]{:S(2)}) copy-start(bf16[4,256,12,128]{3,2,1,0:T(8,128)(2,1)} %reshape.144) | copy-start | bytes 9437188
  136.6 1.6 copy-start.1
  139.9 19.8 %collective-permute-start = (bf16[1,256,1536]{2,1,0:T(8,128)(2,1)S(1)}, bf16[1,256,1536]{2,1,0:T(8,128)(2,1)S(1)}, u32[]{:S(2)}, u32[]{:S(2)}) collective-permute-start(bf16[1,256,1536]{2,1,0:T(8,128)(2,1)S(1)} %fusion.8), channel_id=1, source_target_pairs={{16,0},{0,16},{17,1},{1,17},{18,2},{2,18},{19,3},{3,19},{20,4},{4,... | collective-permute-start | bytes 2359304 | tf_op jit(solution)/shard_map/ppermute | solution.py:14
Sparse Core Ops, SparseCore 0:
  9.7 42.4 all-gather.3
  54.4 52.2 all-gather.5
where the time goes:
time: 168 us; the launch traced here: 167 us
  waiting for transfers between devices  107 us (64%)
  local copies, waits for them, and re-layouts  24.9 us (15%)
  matrix products  14 us (8%)
  between operations  13.6 us (8%)
  other arithmetic  6.35 us (4%)
    all_gather x1, waiting for transfers between devices, local(): lax.all_gather(kv_weight[0], 'frames', axis=1, tiled=True)  48.5 us
    all_gather x1, waiting for transfers between devices, local(): feature_table = lax.all_gather(features, 'frames', axis=0, tiled=True)  38.9 us
    ppermute x1, waiting for transfers between devices, from_behind(): return lax.ppermute(block, axis, route)  18.2 us
    dot_general x1, matrix products, local(): jnp.dot(selected, lax.all_gather(kv_weight[0], 'frames', axis=1, tiled=Tr...  7.88 us
    another operation x1, local copies, waits for them, and re-layouts, local(): values_part = value_heads.reshape(blocks_here, -1, HEADS, HD)  6.87 us
    gather x1, local copies, waits for them, and re-layouts, local(): selected = jnp.take(feature_table, row_index, axis=0)  6.08 us
    dot_general x1, matrix products, local(): jnp.einsum('bqhd,bkhd->bhqk', queries, keys_part, preferred_element_type=...  3.72 us
    another operation x1, local copies, waits for them, and re-layouts, local(): keys_part = key_heads.reshape(blocks_here, -1, HEADS, HD)  3.63 us
  transfers between devices with their start and end apart: 3, of which 3 were waited for; matrix products, arithmetic and copies ran while one was open for 7% of the time, Pallas kernels for 0%

commit v1 on v0

--- a/solution.py
+++ b/solution.py
@@ -1,11 +1,313 @@
+import functools
+
 import jax
 import jax.numpy as jnp
 from jax import lax
+from jax.experimental import pallas as pl
+from jax.experimental.pallas import tpu as pltpu
 from jax.sharding import PartitionSpec as P
 
 HEADS = 12
 HD = 128
 BLK = 64
+MESH = pl.DeviceIdType.MESH
+LINE, LANES, CORES = 4, 2, 2
+GROUPS = 4
+GH = HEADS // GROUPS
+GW = GH * HD
+NT_DIMS = (((1,), (1,)), ((), ()))
+
+
+def tick_kernel(
+    segs,
+    hidden_ref, feat_ref, w_ref, mod_ref, ts_ref, list_ref, count_ref,
+    out_ref,
+    fbuf, wbuf, kbuf, vbuf, qbuf, gbuf, res,
+    zsem, ysem, csem, rsem, osend, orecv,
+):
+    me = lax.axis_index("frames")
+    seg = lax.axis_index("segment")
+    c = me % CORES
+    y = (me // CORES) % LANES
+    z = me // (CORES * LANES)
+    nxt = (seg + 1) % segs
+    half = wbuf.shape[1]
+    nblk = hidden_ref.shape[1] // BLK
+
+    def shard(zz, yy, cc):
+        return (zz * LANES + yy) * CORES + cc
+
+    def slot(p, s):
+        return fbuf.at[s] if p == 0 else wbuf.at[2 * s + (p - 1)]
+
+    def copy(p, s, to, sem):
+        return pltpu.make_async_remote_copy(
+            src_ref=slot(p, s), dst_ref=slot(p, s), send_sem=sem,
+            recv_sem=rsem.at[p, s], device_id={"frames": to}, device_id_type=MESH,
+        )
+
+    def z_copy(p, s, t, up):
+        return copy(p, s, shard(z + 1 if up else z - 1, y, c), zsem.at[p, t, int(up)])
+
+    def y_copy(p, zz):
+        return copy(p, shard(zz, y, c), shard(z, 1 - y, c), ysem.at[p, zz])
+
+    def c_copy(p, zz, yy):
+        return copy(p, shard(zz, yy, c), shard(z, y, 1 - c), csem.at[p, zz * LANES + yy])
+
+    def wait_recv(p, s):
+        copy(p, s, me, csem.at[0, 0]).wait_recv()
+
+    def z_event(p, t):
+        if t == 0:
+            @pl.when(z > 0)
+            def _():
+                z_copy(p, me, 0, False).start()
+
+            @pl.when(z < LINE - 1)
+            def _():
+                z_copy(p, me, 0, True).start()
+
+            y_copy(p, z).start()
+            c_copy(p, z, y).start()
+            return
+
+        @pl.when(z - t >= 0)
+        def _():
+            s = shard(z - t, y, c)
+            wait_recv(p, s)
+
+            @pl.when(z < LINE - 1)
+            def _():
+                z_copy(p, s, t, True).start()
+
+            y_copy(p, z - t).start()
+            c_copy(p, z - t, y).start()
+
+        @pl.when(z + t <= LINE - 1)
+        def _():
+            s = shard(z + t, y, c)
+            wait_recv(p, s)
+
+            @pl.when(z > 0)
+            def _():
+                z_copy(p, s, t, False).start()
+
+            y_copy(p, z + t).start()
+            c_copy(p, z + t, y).start()
+
+    def y_event(p, t):
+        def arrive(zz):
+            wait_recv(p, shard(zz, 1 - y, c))
+            c_copy(p, zz, 1 - y).start()
+
+        if t == 0:
+            arrive(z)
+            return
+
+        @pl.when(z - t >= 0)
+        def _():
+            arrive(z - t)
+
+        @pl.when(z + t <= LINE - 1)
+        def _():
+            arrive(z + t)
+
+    def from_core(p, zz, yy):
+        wait_recv(p, shard(zz, yy, 1 - c))
+
+    def queries():
+        def one(b, carry):
+            rows = pl.ds(pl.multiple_of(b * BLK, BLK), BLK)
+            x = hidden_ref[0, rows, :].astype(jnp.float32)
+            normed = x * lax.rsqrt(jnp.mean(x * x, axis=-1, keepdims=True) + 1e-06)
+            mod = mod_ref[0, ts_ref[0, b]]
+            q = (normed * (1.0 + mod[1:2]) + mod[0:1]).astype(jnp.bfloat16)
+            for g in range(GROUPS):
+                qbuf[g, rows, :] = q[:, g * GW:(g + 1) * GW]
+                gbuf[g, b] = mod[2:3, g * GW:(g + 1) * GW]
+            return carry
+
+        lax.fori_loop(0, nblk, one, 0)
+
+    def group(zz, yy):
+        g = zz * LANES + yy
+        keys = wbuf[pl.ds(4 * g, 4)].reshape(4 * half, wbuf.shape[2])
+        values = wbuf[pl.ds(16 + 4 * g, 4)].reshape(4 * half, wbuf.shape[2])
+        step = 4
+        rows_step = step * fbuf.shape[1]
+
+        def project(r, carry):
+            f = fbuf[pl.ds(r * step, step)].reshape(rows_step, fbuf.shape[2])
+            for buf, weight in ((kbuf, keys), (vbuf, values)):
+                part = lax.dot_general(f, weight, NT_DIMS, preferred_element_type=jnp.float32)
+                buf[pl.ds(r * step, step)] = part.astype(jnp.bfloat16).reshape(step, BLK, GW)
+            return carry
+
+        lax.fori_loop(0, fbuf.shape[0] // step, project, 0)
+        sel = list_ref.shape[2]
+        columns = pl.ds(pl.multiple_of(g * GW, GW), GW)
+
+        def attend(b):
+            rows = pl.ds(pl.multiple_of(b * BLK, BLK), BLK)
+            k = jnp.concatenate([kbuf[list_ref[0, b, j]] for j in range(sel)], axis=0)
+            v = jnp.concatenate([vbuf[list_ref[0, b, j]] for j in range(sel)], axis=0)
+            live = lax.broadcasted_iota(jnp.int32, (BLK, sel * BLK), 1) < count_ref[0, b] * BLK
+            q = qbuf[g, rows, :]
+            mixed = []
+            for h in range(GH):
+                part = slice(h * HD, (h + 1) * HD)
+                scores = lax.dot_general(
+                    q[:, part], k[:, part], NT_DIMS, preferred_element_type=jnp.float32
+                )
+                scores = jnp.where(live, scores * (1.0 / HD ** 0.5), jnp.float32(-1e30))
+                expo = jnp.exp(scores - jnp.max(scores, axis=-1, keepdims=True))
+                weights = (expo / jnp.sum(expo, axis=-1, keepdims=True)).astype(jnp.bfloat16)
+                mixed.append(jnp.dot(weights, v[:, part], preferred_element_type=jnp.float32))
+            x = hidden_ref[0, rows, columns].astype(jnp.float32)
+            res[g, rows, :] = (x + gbuf[g, b] * jnp.concatenate(mixed, axis=1)).astype(
+                jnp.bfloat16
+            )
+
+        def pair(i, carry):
+            attend(2 * i)
+            attend(2 * i + 1)
+            return carry
+
+        lax.fori_loop(0, nblk // 2, pair, 0)
+        hand(g).start()
+
+    def hand(g):
+        columns = pl.ds(pl.multiple_of(g * GW, GW), GW)
+        return pltpu.make_async_remote_copy(
+            src_ref=res.at[g], dst_ref=out_ref.at[0, :, columns], send_sem=osend.at[g],
+            recv_sem=orecv.at[g], device_id={"segment": nxt}, device_id_type=MESH,
+        )
+
+    fbuf[me] = feat_ref[...]
+    barrier = pltpu.get_barrier_semaphore()
+
+    def greet(**where):
+        pl.semaphore_signal(barrier, inc=1, device_id=where, device_id_type=MESH)
+
+    @pl.when(z > 0)
+    def _():
+        greet(frames=shard(z - 1, y, c))
+
+    @pl.when(z < LINE - 1)
+    def _():
+        greet(frames=shard(z + 1, y, c))
+
+    greet(frames=shard(z, 1 - y, c))
+    greet(frames=shard(z, y, 1 - c))
+    greet(segment=nxt)
+    if segs > 2:
+        greet(segment=(seg + segs - 1) % segs)
+    ends = jnp.where(z == 0, 1, 0) + jnp.where(z == LINE - 1, 1, 0)
+    pl.semaphore_wait(barrier, (5 if segs > 2 else 4) + 1 - ends)
+
+    z_event(0, 0)
+    turned = w_ref[0].T
+    wbuf[2 * me] = turned[:half]
+    wbuf[2 * me + 1] = turned[half:]
+    z_event(1, 0)
+    queries()
+    z_event(0, 1)
+    z_event(2, 0)
+    z_event(0, 2)
+    z_event(1, 1)
+    y_event(0, 0)
+    z_event(0, 3)
+    z_event(2, 1)
+    y_event(0, 1)
+    y_event(0, 2)
+    z_event(1, 2)
+    y_event(1, 0)
+    z_event(2, 2)
+    y_event(0, 3)
+    y_event(2, 0)
+    for zz in range(LINE):
+        for yy in range(LANES):
+            from_core(0, zz, yy)
+
+    def from_core_pair(zz, yy):
+        for p in (1, 2):
+            from_core(p, zz, yy)
+            from_core(p, zz + LANES, yy)
+
+    first, other = z % 2, 1 - z % 2
+    from_core_pair(first, y)
+    group(first, y)
+    z_event(1, 3)
+    y_event(1, 1)
+    z_event(2, 3)
+    y_event(2, 1)
+    from_core_pair(other, y)
+    group(other, y)
+    y_event(1, 2)
+    y_event(2, 2)
+    from_core_pair(first, 1 - y)
+    group(first, 1 - y)
+    y_event(1, 3)
+    y_event(2, 3)
+    from_core_pair(other, 1 - y)
+    group(other, 1 - y)
+
+    for p in range(3):
+        for t in range(LINE - 1):
+            @pl.when((z - t >= 0) & (z < LINE - 1))
+            def _():
+                z_copy(p, me, t, True).wait_send()
+
+            @pl.when((z + t <= LINE - 1) & (z > 0))
+            def _():
+                z_copy(p, me, t, False).wait_send()
+
+        for zz in range(LINE):
+            y_copy(p, zz).wait_send()
+            for yy in range(LANES):
+                c_copy(p, zz, yy).wait_send()
+    for g in range(GROUPS):
+        hand(g).wait()
+
+
+def local_line(segs, hidden, features, kv_weight, mod_table, timestep, block_list, block_count):
+    n = LINE * LANES * CORES
+    rows, width = hidden.shape[1:]
+    frows, fwidth = features.shape
+    half = kv_weight.shape[2] // 2
+    nblk = rows // BLK
+    vmem = pl.BlockSpec(memory_space=pltpu.VMEM)
+    smem = pl.BlockSpec(memory_space=pltpu.SMEM)
+    bf16 = jnp.bfloat16
+    return pl.pallas_call(
+        functools.partial(tick_kernel, segs),
+        out_shape=jax.ShapeDtypeStruct(hidden.shape, bf16),
+        in_specs=[vmem, vmem, vmem, vmem, smem, smem, smem],
+        out_specs=pl.BlockSpec(memory_space=pl.ANY),
+        scratch_shapes=[
+            pltpu.VMEM((n, frows, fwidth), bf16),
+            pltpu.VMEM((2 * n, half, fwidth), bf16),
+            pltpu.VMEM((n * frows // BLK, BLK, GW), bf16),
+            pltpu.VMEM((n * frows // BLK, BLK, GW), bf16),
+            pltpu.VMEM((GROUPS, rows, GW), bf16),
+            pltpu.VMEM((GROUPS, nblk, 1, GW), jnp.float32),
+            pltpu.VMEM((GROUPS, rows, GW), bf16),
+            pltpu.SemaphoreType.DMA((3, LINE, 2)),
+            pltpu.SemaphoreType.DMA((3, LINE)),
+            pltpu.SemaphoreType.DMA((3, LINE * LANES)),
+            pltpu.SemaphoreType.DMA((3, n)),
+            pltpu.SemaphoreType.DMA((GROUPS,)),
+            pltpu.SemaphoreType.DMA((GROUPS,)),
+        ],
+        compiler_params=pltpu.CompilerParams(
+            collective_id=0, has_side_effects=True, vmem_limit_bytes=40 * 1024 * 1024
+        ),
+        cost_estimate=pl.CostEstimate(
+            flops=2 * n * frows * fwidth * 2 * width, bytes_accessed=1 << 24,
+            transcendentals=rows * 4 * BLK * HEADS,
+        ),
+    )(hidden, features, kv_weight, mod_table, timestep, block_list, block_count)
 
 
 def from_behind(block, axis, distance):
@@ -79,6 +381,9 @@
         P("segment", "frames", None),
         P("segment", "frames"),
     )
+    step = local
+    if mesh.shape["frames"] == LINE * LANES * CORES:
+        step = functools.partial(local_line, mesh.shape["segment"])
     return jax.shard_map(
-        local, mesh=mesh, in_specs=placed, out_specs=P("segment", "frames", None), check_vma=False
-    )
+        step, mesh=mesh, in_specs=placed, out_specs=P("segment", "frames", None), check_vma=False
+    )

time: 168 us -> 67 us (0.40)
  waiting for transfers between devices: 107 us -> 0 us
  Pallas kernels: 0 us -> 63.6 us
  local copies, waits for them, and re-layouts: 24.9 us -> 3.18 us
  matrix products: 14 us -> 0 us
  between operations: 13.6 us -> 0.07 us
  other arithmetic: 6.35 us -> 0 us
    all_gather x2 -> x0, waiting for transfers between devices: 87.4 us -> none  [the longest x1 48.5 us: local(): lax.all_gather(kv_weight[0], 'frames', axis=1, tiled=True)]
    pallas_call x0 -> x1, Pallas kernels: none -> 63.6 us  [local_line(): pl.pallas_call(functools.partial(tick_kernel, segs), out_shape=jax.ShapeD...]
    ppermute x1 -> x0, waiting for transfers between devices: 18.2 us -> none  [from_behind(): return lax.ppermute(block, axis, route)]
    dot_general x3 -> x0, matrix products: 14 us -> none  [the longest x1 7.88 us: local(): jnp.dot(selected, lax.all_gather(kv_weight[0], 'frames', axis=1, tiled=Tr...]
    another operation x2 -> x0, local copies, waits for them, and re-layouts: 10.5 us -> none  [the longest x1 6.87 us: local(): values_part = value_heads.reshape(blocks_here, -1, HEADS, HD)]
    gather x1 -> x0, local copies, waits for them, and re-layouts: 6.08 us -> none  [local(): selected = jnp.take(feature_table, row_index, axis=0)]
    convert_element_type x3 -> x0, other arithmetic: 3.31 us -> none  [the longest x1 1.8 us: local(): result = (stream + gate_rows * mixed_rows).astype(jnp.bfloat16)]
    slice x1 -> x0, local copies, waits for them, and re-layouts: 2.17 us -> none  [local(): key_heads = key_values[:, :feature_width].reshape(-1, HEADS, HD)]
  transfers between devices with their start and end apart: 3 -> 0, of which waited for: 3 -> 0; matrix products, arithmetic and copies ran while one was open for 7% -> 0% of each run, Pallas kernels for 0% -> 0%
where the time goes in v1:
time: 67 us; the launch traced here: 66.9 us
  Pallas kernels  63.6 us (95%)
  local copies, waits for them, and re-layouts  3.18 us (5%)
    pallas_call x1, Pallas kernels, local_line(): pl.pallas_call(functools.partial(tick_kernel, segs), out_shape=jax.ShapeD...  63.6 us
    unnamed x15, local copies, waits for them, and re-layouts  3.18 us

profile of v1, /device:TPU:0, one launch (start us, length us, event | category | flops | bytes accessed | tf_op | source)
XLA Modules:
  0.0 66.9 jit_solution(16707444844553997589)
XLA Ops:
  0.0 0.0 copy-start.5
  0.0 1.2 %copy.8.w_ref = bf16[1,768,192]{2,1,0:T(8,128)(2,1)S(1)} copy(bf16[1,768,192]{1,2,0:T(8,128)(2,1)} %param.9) | data formatting | bytes 589824 | tf_op args[2]
  1.2 0.0 copy-done.5
  1.2 0.0 copy-start
  1.2 0.0 copy-start.1
  1.2 0.0 copy-start.2
  1.2 0.0 copy-start.3
  1.3 0.0 copy-start.4
  1.3 0.4 copy.9.mod_ref
  1.7 0.7 copy-done
  2.3 0.0 copy-done.1
  2.3 0.0 copy-done.2
  2.4 0.0 copy-done.3
  2.4 0.0 copy-done.4
  2.4 63.6 %shard_map.73 = bf16[1,256,1536]{2,1,0:T(8,128)(2,1)S(1)} custom-call(bf16[1,256,1536]{2,1,0:T(8,128)(2,1)S(1)} %copy-done, bf16[64,768]{1,0:T(8,128)(2,1)S(1)} %copy-done.1, bf16[1,768,192]{2,1,0:T(8,128)(2,1)S(1)} %copy.8.w_ref, f32[1,32,3,1536]{3,2,1,0:T(4,128)S(1)} %copy.9.mod_ref, s32[1,4]{1,0:T(1,128)S(1)} %copy-done.3, s32[1,4,4]{2,1,0:T(4,128)S(1)} %copy-done.2, ...), custom_call_target="tpu_custom_call" | custom-call | flops 4831838208 | bytes 16777216 | tf_op jit(solution)/shard_map/pallas_call | solution.py:283
  66.0 0.9 %copy.11 = bf16[1,256,1536]{2,1,0:T(8,128)(2,1)} copy(bf16[1,256,1536]{2,1,0:T(8,128)(2,1)S(1)} %shard_map.73) | data formatting | bytes 1572864
Async XLA Ops:
  0.0 1.2 %copy-start.5 = (f32[1,32,3,1536]{3,1,2,0:T(8,128)S(1)}, f32[1,32,3,1536]{3,1,2,0:T(8,128)}, u32[]{:S(2)}) copy-start(f32[1,32,3,1536]{3,1,2,0:T(8,128)} %param.10) | copy-start | bytes 1769476
  1.2 1.1 %copy-start = (bf16[1,256,1536]{2,1,0:T(8,128)(2,1)S(1)}, bf16[1,256,1536]{2,1,0:T(8,128)(2,1)}, u32[]{:S(2)}) copy-start(bf16[1,256,1536]{2,1,0:T(8,128)(2,1)} %hidden_ref.1) | copy-start | bytes 2359300
  1.2 1.1 %copy-start.1 = (bf16[64,768]{1,0:T(8,128)(2,1)S(1)}, bf16[64,768]{1,0:T(8,128)(2,1)}, u32[]{:S(2)}) copy-start(bf16[64,768]{1,0:T(8,128)(2,1)} %feat_ref.1) | copy-start | bytes 294916
  1.2 1.1 %copy-start.2 = (s32[1,4,4]{2,1,0:T(4,128)S(1)}, s32[1,4,4]{2,1,0:T(4,128)}, u32[]{:S(2)}) copy-start(s32[1,4,4]{2,1,0:T(4,128)} %list_ref.1) | copy-start | bytes 196
  1.2 1.1 %copy-start.3 = (s32[1,4]{1,0:T(1,128)S(1)}, s32[1,4]{1,0:T(1,128)}, u32[]{:S(2)}) copy-start(s32[1,4]{1,0:T(1,128)} %ts_ref.1) | copy-start | bytes 52
  1.3 1.1 %copy-start.4 = (s32[1,4]{1,0:T(1,128)S(1)}, s32[1,4]{1,0:T(1,128)}, u32[]{:S(2)}) copy-start(s32[1,4]{1,0:T(1,128)} %count_ref.1) | copy-start | bytes 52
